TPU v7x, 32 devices: a whole 2x2x4 slice. The times are simulated.
32 devices in a mesh: rows: 8 (over z, x), chan: 4 (over y, core).
Axes of the slice: x: 2, y: 2, z: 4, core: 2. Of those that a mesh axis runs over, the one named last changes fastest.
Arguments:
- inputs: bfloat16 [256, 16, 1024], P('chan', 'rows'), may hold values from -6 to 6
- kernel: bfloat16 [256, 2304], replicated, may hold values from -0.125 to 0.125
- out_grad: bfloat16 [256, 16, 1024], P('chan', 'rows'), may hold values from -6 to 6
Outputs:
- outputs: bfloat16 [256, 16, 1024], P('chan', 'rows')
- in_grad: bfloat16 [256, 16, 1024], P('chan', 'rows')
- kernel_grad: float32 [256, 2304], P('chan', 'rows')
All inputs are finite; a program needn't handle non-finite values.
Results may differ from a plain program's by a relative error of at most 0.00105.
Values may be sent and summed in bfloat16 or wider, within the bound.
A program may use at most 64 MiB of HBM per device.

v0:
```python
import math

import jax
import jax.numpy as jnp
from jax import lax
from jax.sharding import PartitionSpec as P


def with_halo(x, sides, width):
    for axis, dim in sides:
        count, length = (lax.axis_size(axis), x.shape[dim])
        up = [(i, (i + 1) % count) for i in range(count - 1)]
        down = [(j, i) for i, j in up]
        last = lax.slice_in_dim(x, length - width, length, axis=dim)
        initial = lax.slice_in_dim(x, 0, width, axis=dim)
        before = lax.ppermute(last, axis, up)
        after = lax.ppermute(initial, axis, down)
        x = jnp.concatenate([before, x, after], axis=dim)
    return x


def convolve(source, filters, specs):
    return lax.conv_general_dilated(
        source,
        filters,
        (1, 1),
        ((0, 0), (1, 1)),
        dimension_numbers=specs,
        preferred_element_type=jnp.float32,
    )


def body(inputs, kernel, out_grad):
    channels = kernel.shape[0]
    own_count = inputs.shape[0]
    height = inputs.shape[1]
    breadth = inputs.shape[2]
    first = lax.axis_index("chan") * own_count
    taps = kernel.reshape(channels, 3, 3, channels)
    whole_in = lax.all_gather(inputs, "chan", axis=0, tiled=True)
    padded_in = with_halo(whole_in, (("rows", 1),), 1)
    own_taps = lax.dynamic_slice_in_dim(taps, first, own_count, 0)
    outputs = convolve(padded_in[None], own_taps, ("NCHW", "OHWI", "NCHW"))[0].astype(jnp.bfloat16)
    own_padded = with_halo(out_grad, (("rows", 1),), 1)
    picked = own_taps[:, ::-1, ::-1, :]
    in_grad = lax.psum_scatter(
        convolve(own_padded[None], picked, ("NCHW", "IHWO", "NCHW"))[0],
        "chan",
        scatter_dimension=0,
        tiled=True,
    ).astype(jnp.bfloat16)
    kernel_terms = convolve(padded_in[None], out_grad[None], ("CNHW", "IOHW", "CNHW"))
    local_grad = jnp.transpose(kernel_terms, (0, 2, 3, 1)).reshape(own_count, 9 * channels)
    strips = lax.axis_size("rows")
    piece = 9 * channels // strips
    blocks = jnp.transpose(local_grad.reshape(own_count, strips, piece), (1, 0, 2))
    summed = lax.psum_scatter(blocks, "rows", scatter_dimension=0, tiled=True).reshape(
        own_count, piece
    )
    scale = 1.0 / math.sqrt(height * strips * breadth)
    return (outputs, in_grad, summed * scale)


def solution(mesh):
    placed = (P("chan", "rows", None), P(), P("chan", "rows", None))
    return jax.shard_map(
        body,
        mesh=mesh,
        in_specs=placed,
        out_specs=(P("chan", "rows", None), P("chan", "rows", None), P("chan", "rows")),
        check_vma=False,
    )
```

profile of v0, /device:TPU:11, one launch (start us, length us, event | category | flops | bytes accessed | tf_op | source)
XLA Modules:
  0.0 168.1 jit_solution(762662748249277659)
XLA Ops:
  7.2 1.8 %copy.41 = bf16[64,2,1024]{2,0,1:T(8,128)(2,1)} copy(bf16[64,2,1024]{2,1,0:T(2,128)(2,1)} %param.3) | data formatting | bytes 524288 | tf_op args[0]
  9.1 2.3 %fusion.28 = (bf16[64,1,1024]{2,1,0:T(2,128)(2,1)}, bf16[64,1,1024]{2,1,0:T(2,128)(2,1)}) fusion(bf16[64,2,1024]{2,1,0:T(2,128)(2,1)} %param.5), kind=kLoop, calls=%fused_computation.38 | loop fusion | bytes 524288 | tf_op jit(solution)/shard_map/slice | solution.py:14
  11.4 3.3 %collective-permute-start.2 = (bf16[64,1,1024]{2,1,0:T(2,128)(2,1)}, bf16[64,1,1024]{2,1,0:T(2,128)(2,1)S(1)}, u32[]{:S(2)}, u32[]{:S(2)}) collective-permute-start(bf16[64,1,1024]{2,1,0:T(2,128)(2,1)} %get-tuple-element.14), channel_id=1, source_target_pairs={{0,4},{4,8},{8,12},{12,16},{16,20},{20,24},{24,28},{1,5},{5,9},{9,... | collective-permute-start | bytes 393224 | tf_op jit(solution)/shard_map/ppermute | solution.py:16
  14.7 2.1 %collective-permute-start.3 = (bf16[64,1,1024]{2,1,0:T(2,128)(2,1)}, bf16[64,1,1024]{2,1,0:T(2,128)(2,1)S(1)}, u32[]{:S(2)}, u32[]{:S(2)}) collective-permute-start(bf16[64,1,1024]{2,1,0:T(2,128)(2,1)} %get-tuple-element.15), channel_id=1, source_target_pairs={{4,0},{8,4},{12,8},{16,12},{20,16},{24,20},{28,24},{5,1},{9,5},{13... | collective-permute-start | bytes 393224 | tf_op jit(solution)/shard_map/ppermute | solution.py:17
  17.5 2.2 %copy.56 = bf16[1,64,2,1024]{1,0,3,2:T(2,128)(2,1)} copy(bf16[1,64,2,1024]{3,2,1,0:T(2,128)(2,1)S(1)} %bitcast.38) | data formatting | bytes 524288 | tf_op jit(solution)/shard_map/broadcast_in_dim | solution.py:52
  20.9 5.6 %collective-permute-done.2 = bf16[64,1,1024]{2,1,0:T(2,128)(2,1)S(1)} collective-permute-done((bf16[64,1,1024]{2,1,0:T(2,128)(2,1)}, bf16[64,1,1024]{2,1,0:T(2,128)(2,1)S(1)}, u32[]{:S(2)}, u32[]{:S(2)}) %collective-permute-start.2) | collective-permute-done | bytes 131104 | tf_op jit(solution)/shard_map/ppermute | solution.py:16
  29.3 2.3 %copy.52 = bf16[64,4,1,8,129]{0,3,4,1,2:T(8,128)(2,1)} copy(bf16[64,4,1,8,129]{4,3,1,0,2:T(8,128)(2,1)S(1)} %reshape.40) | data formatting | bytes 1056768 | tf_op jit(solution)/shard_map/conv_general_dilated | solution.py:23
  32.5 2.3 %fusion.27 = (bf16[256,1,1024]{2,0,1:T(8,128)(2,1)}, bf16[256,1,1024]{2,0,1:T(8,128)(2,1)}) fusion(bf16[256,2,1024]{2,0,1:T(8,128)(2,1)} %all-gather.2.cloned.1.call-done), kind=kLoop, calls=%fused_computation.37 | loop fusion | bytes 2097152 | tf_op jit(solution)/shard_map/slice | solution.py:15
  34.8 5.0 %collective-permute-start = (bf16[256,1,1024]{2,0,1:T(8,128)(2,1)}, bf16[256,1,1024]{2,0,1:T(8,128)(2,1)}, u32[]{:S(2)}, u32[]{:S(2)}) collective-permute-start(bf16[256,1,1024]{2,0,1:T(8,128)(2,1)} %get-tuple-element.13), channel_id=1, source_target_pairs={{0,4},{4,8},{8,12},{12,16},{16,20},{20,24},{24,28},{1,5},{5,9},{9,... | collective-permute-start | bytes 1572872 | tf_op jit(solution)/shard_map/ppermute | solution.py:16
  39.8 1.7 %convolution_select_fusion = f32[2,8,129,256]{3,1,2,0:T(8,128)S(1)} fusion(bf16[64,4,1,7,2]{0,3,4,1,2:T(8,128)(2,1)S(1)} %slice.24, bf16[64,4,1,8,129]{0,3,4,1,2:T(8,128)(2,1)S(1)} %copy-done.5, pred[8,129]{0,1:T(8,128)(4,1)S(1)} %copy-done.8, bf16[256,3,3,256]{0,3,2,1:T(8,128)(2,1)S(1)} %bitcast.40, s32[]{:T(128)S(6)} %select_n.3), kind=kOutput, calls=%fused_computation.11 | convolution fusion | flops 610836480 | bytes 3793924 | tf_op jit(solution)/shard_map/conv_general_dilated | solution.py:23
  42.1 1.6 reshape.27
  43.8 1.9 %collective-permute-start.1 = (bf16[256,1,1024]{2,0,1:T(8,128)(2,1)}, bf16[256,1,1024]{2,0,1:T(8,128)(2,1)}, u32[]{:S(2)}, u32[]{:S(2)}) collective-permute-start(bf16[256,1,1024]{2,0,1:T(8,128)(2,1)} %get-tuple-element.12), channel_id=1, source_target_pairs={{4,0},{8,4},{12,8},{16,12},{20,16},{24,20},{28,24},{5,1},{9,5},{13... | collective-permute-start | bytes 1572872 | tf_op jit(solution)/shard_map/ppermute | solution.py:17
  45.7 1.7 %slice_bitcast_fusion = f32[256,2,1024]{0,2,1:T(8,128)S(1)} fusion(f32[2,1,1032,256]{3,2,0,1:T(8,128)} %reshape.27), kind=kLoop, calls=%fused_computation.10 | loop fusion | bytes 4194304 | tf_op jit(solution)/shard_map/squeeze | solution.py:47
  47.4 2.4 %copy.54 = f32[256,2,1024]{2,1,0:T(2,128)} copy(f32[256,2,1024]{0,2,1:T(8,128)S(1)} %slice_bitcast_fusion) | data formatting | bytes 4194304 | tf_op jit(solution)/shard_map/squeeze | solution.py:47
  49.8 11.7 %collective-permute-done = bf16[256,1,1024]{2,0,1:T(8,128)(2,1)} collective-permute-done((bf16[256,1,1024]{2,0,1:T(8,128)(2,1)}, bf16[256,1,1024]{2,0,1:T(8,128)(2,1)}, u32[]{:S(2)}, u32[]{:S(2)}) %collective-permute-start) | collective-permute-done | bytes 524320 | tf_op jit(solution)/shard_map/ppermute | solution.py:16
  63.9 7.4 %copy.55 = bf16[1,256,4,1024]{1,0,3,2:T(2,128)(2,1)} copy(bf16[1,256,4,1024]{3,1,2,0:T(8,128)(2,1)S(1)} %bitcast.36) | data formatting | bytes 4194304 | tf_op jit(solution)/shard_map/broadcast_in_dim | solution.py:43
  71.3 15.9 %fusion.29 = f32[64,3,3,256]{3,0,2,1:T(8,128)S(1)} fusion(bf16[1,256,4,1024]{1,0,3,2:T(2,128)(2,1)} %copy.55, bf16[1,64,2,1024]{1,0,3,2:T(2,128)(2,1)S(1)} %copy-done.6), kind=kOutput, calls=%fused_computation.39 | convolution fusion | flops 603586560 | bytes 2949120 | tf_op jit(solution)/shard_map/transpose | solution.py:53
  88.5 1.9 %reshape_reshape.3 = f32[64,8,288]{2,1,0:T(8,128)S(1)} reshape(f32[64,3,3,256]{3,2,1,0:T(4,128)} %copy.57) | data formatting | bytes 1179648 | tf_op jit(solution)/shard_map/reshape;reshape | solution.py:56
  91.5 42.2 %all-reduce.2 = bf16[256,2,1024]{2,1,0:T(2,128)(2,1)S(1)} all-reduce(f32[256,2,1024]{2,1,0:T(2,128)} %copy.54), channel_id=2, replica_groups=mesh['rows'=8,'chan'=4] {'chan'}, use_global_device_ids=true, to_apply=%region_0.0.clone | all-reduce | flops 524288 | bytes 3145728
  134.6 2.7 %pad = bf16[256,4,1,1032]{3,0,1,2:T(8,128)(2,1)} pad(bf16[256,4,1,1024]{3,0,1,2:T(8,128)(2,1)S(1)} %bitcast.37, bf16[]{:T(256)} %constant.14), padding=0_0x0_0x0_0x1_7 | pad | bytes 4210690 | tf_op jit(solution)/shard_map/broadcast_in_dim | solution.py:43
  137.3 8.5 %reshape.39 = bf16[256,4,1,8,129]{4,3,0,1,2:T(8,128)(2,1)} reshape(bf16[256,4,1,1032]{3,0,1,2:T(8,128)(2,1)} %pad) | data formatting | bytes 4227072 | tf_op jit(solution)/shard_map/conv_general_dilated | solution.py:23
  145.8 7.0 %copy.44 = bf16[256,4,1,8,129]{0,3,4,1,2:T(8,128)(2,1)S(1)} copy(bf16[256,4,1,8,129]{4,3,0,1,2:T(8,128)(2,1)} %reshape.39) | data formatting | bytes 4227072 | tf_op jit(solution)/shard_map/conv_general_dilated | solution.py:23
  152.9 3.5 %fusion.3 = bf16[2,8,129,64]{3,1,2,0:T(8,128)(2,1)} fusion(bf16[256,4,1,7,2]{0,3,4,1,2:T(8,128)(2,1)S(1)} %slice.22, bf16[256,4,1,8,129]{0,3,4,1,2:T(8,128)(2,1)S(1)} %copy.44, bf16[256,3,3,256]{0,3,2,1:T(8,128)(2,1)S(1)} %bitcast.41, s32[]{:T(128)S(6)} %select_n.3), kind=kOutput, calls=%fused_computation.4 | convolution fusion | flops 615137280 | bytes 3000324 | tf_op jit(solution)/shard_map/conv_general_dilated | solution.py:23
  159.7 1.5 multiply_bitcast_fusion
  (48 shorter events, 14.5 us)
Async XLA Ops:
  7.2 10.3 %copy-start = (bf16[64,2,1024]{2,1,0:T(2,128)(2,1)S(1)}, bf16[64,2,1024]{2,1,0:T(2,128)(2,1)}, u32[]{:S(2)}) copy-start(bf16[64,2,1024]{2,1,0:T(2,128)(2,1)} %param.5) | copy-start | bytes 786436
  7.2 9.6 %copy-start.2 = (bf16[256,2304]{1,0:T(8,128)(2,1)S(1)}, bf16[256,2304]{1,0:T(8,128)(2,1)}, u32[]{:S(2)}) copy-start(bf16[256,2304]{1,0:T(8,128)(2,1)} %param.4) | copy-start | bytes 3538948
  7.2 25.3 %all-gather.2.cloned.1.call-start = ((), (), s32[]{:S(2)}) async-start(), calls=%async_computation.1 | async-start | bytes 1310720 | tf_op jit(solution)/shard_map/all_gather | solution.py:40
  9.1 150.6 %reduce-scatter.2.cloned.1.call-start = ((), (), s32[]{:S(2)}) async-start(), calls=%async_computation.2 | async-start | bytes 884736 | tf_op jit(solution)/shard_map/reduce_scatter | solution.py:57
  11.4 8.3 %copy-start.9 = (u32[32]{0:T(128)S(1)}, u32[32]{0:T(128)}, u32[]{:S(2)}) copy-start(u32[32]{0:T(128)} %constant.26) | copy-start | bytes 388
  11.4 15.1 %collective-permute-start.2 = (bf16[64,1,1024]{2,1,0:T(2,128)(2,1)}, bf16[64,1,1024]{2,1,0:T(2,128)(2,1)S(1)}, u32[]{:S(2)}, u32[]{:S(2)}) collective-permute-start(bf16[64,1,1024]{2,1,0:T(2,128)(2,1)} %get-tuple-element.14), channel_id=1, source_target_pairs={{0,4},{4,8},{8,12},{12,16},{16,20},{20,24},{24,28},{1,5},{5,9},{9,... | collective-permute-start | bytes 393224 | tf_op jit(solution)/shard_map/ppermute | solution.py:16
  14.7 11.8 %collective-permute-start.3 = (bf16[64,1,1024]{2,1,0:T(2,128)(2,1)}, bf16[64,1,1024]{2,1,0:T(2,128)(2,1)S(1)}, u32[]{:S(2)}, u32[]{:S(2)}) collective-permute-start(bf16[64,1,1024]{2,1,0:T(2,128)(2,1)} %get-tuple-element.15), channel_id=1, source_target_pairs={{4,0},{8,4},{12,8},{16,12},{20,16},{24,20},{28,24},{5,1},{9,5},{13... | collective-permute-start | bytes 393224 | tf_op jit(solution)/shard_map/ppermute | solution.py:17
  17.4 22.3 %copy-start.3 = (bf16[256,2304]{0,1:T(8,128)(2,1)}, bf16[256,2304]{0,1:T(8,128)(2,1)S(1)}, u32[]{:S(2)}) copy-start(bf16[256,2304]{0,1:T(8,128)(2,1)S(1)} %copy.45) | copy-start | bytes 3538948
  29.3 10.5 %copy-start.8 = (pred[8,129]{0,1:T(8,128)(4,1)S(1)}, pred[8,129]{0,1:T(8,128)(4,1)}, u32[]{:S(2)}) copy-start(pred[8,129]{0,1:T(8,128)(4,1)} %constant.28) | copy-start | bytes 3100
  31.7 8.1 %copy-start.5 = (bf16[64,4,1,8,129]{0,3,4,1,2:T(8,128)(2,1)S(1)}, bf16[64,4,1,8,129]{0,3,4,1,2:T(8,128)(2,1)}, u32[]{:S(2)}) copy-start(bf16[64,4,1,8,129]{0,3,4,1,2:T(8,128)(2,1)} %copy.52) | copy-start | bytes 1585156
  34.8 26.7 %collective-permute-start = (bf16[256,1,1024]{2,0,1:T(8,128)(2,1)}, bf16[256,1,1024]{2,0,1:T(8,128)(2,1)}, u32[]{:S(2)}, u32[]{:S(2)}) collective-permute-start(bf16[256,1,1024]{2,0,1:T(8,128)(2,1)} %get-tuple-element.13), channel_id=1, source_target_pairs={{0,4},{4,8},{8,12},{12,16},{16,20},{20,24},{24,28},{1,5},{5,9},{9,... | collective-permute-start | bytes 1572872 | tf_op jit(solution)/shard_map/ppermute | solution.py:16
  43.8 19.1 %collective-permute-start.1 = (bf16[256,1,1024]{2,0,1:T(8,128)(2,1)}, bf16[256,1,1024]{2,0,1:T(8,128)(2,1)}, u32[]{:S(2)}, u32[]{:S(2)}) collective-permute-start(bf16[256,1,1024]{2,0,1:T(8,128)(2,1)} %get-tuple-element.12), channel_id=1, source_target_pairs={{4,0},{8,4},{12,8},{16,12},{20,16},{24,20},{28,24},{5,1},{9,5},{13... | collective-permute-start | bytes 1572872 | tf_op jit(solution)/shard_map/ppermute | solution.py:17
  47.4 15.1 %copy-start.1 = (bf16[256,2,1024]{2,0,1:T(8,128)(2,1)S(1)}, bf16[256,2,1024]{2,0,1:T(8,128)(2,1)}, u32[]{:S(2)}) copy-start(bf16[256,2,1024]{2,0,1:T(8,128)(2,1)} %all-gather.2.cloned.1.call-done) | copy-start | bytes 3145732
  63.9 7.4 %copy-start.6 = (bf16[1,64,2,1024]{1,0,3,2:T(2,128)(2,1)S(1)}, bf16[1,64,2,1024]{1,0,3,2:T(2,128)(2,1)}, u32[]{:S(2)}) copy-start(bf16[1,64,2,1024]{1,0,3,2:T(2,128)(2,1)} %copy.56) | copy-start | bytes 786436
  145.8 7.0 %copy-start.4 = (bf16[256,2304]{0,1:T(8,128)(2,1)S(1)}, bf16[256,2304]{0,1:T(8,128)(2,1)}, u32[]{:S(2)}) copy-start(bf16[256,2304]{0,1:T(8,128)(2,1)} %copy-done.3) | copy-start | bytes 3538948
  152.8 4.9 %copy-start.7 = (pred[8,129]{1,0:T(8,128)(4,1)S(1)}, pred[8,129]{1,0:T(8,128)(4,1)}, u32[]{:S(2)}) copy-start(pred[8,129]{1,0:T(8,128)(4,1)} %constant.22) | copy-start | bytes 3100
Sparse Core Ops, SparseCore 0:
  10.2 18.2 all-gather.1
  91.6 62.4 reduce-scatter.1
where the time goes:
time: 171 us; the launch traced here: 168 us
  local copies, waits for them, and re-layouts  57.3 us (34%)
  blocking collectives  42.2 us (25%)
  matrix products  21.1 us (12%)
  waiting for transfers between devices  17.5 us (10%)
  between operations  15 us (9%)
  starting transfers between devices  12.4 us (7%)
  other arithmetic  2.52 us (1%)
    unnamed x1, blocking collectives  42.2 us
    conv_general_dilated x9, local copies, waits for them, and re-layouts, convolve(): lax.conv_general_dilated(source, filters, (1, 1), ((0, 0), (1, 1)), dimen...  23.8 us
    ppermute x2, waiting for transfers between devices, with_halo(): before = lax.ppermute(last, axis, up)  17.3 us
    transpose x1, matrix products, body(): jnp.transpose(kernel_terms, (0, 2, 3, 1)).reshape(own_count, 9 * channels)  15.9 us
    broadcast_in_dim x2, local copies, waits for them, and re-layouts, body(): padded_in[None]  10.1 us
    ppermute x2, starting transfers between devices, with_halo(): before = lax.ppermute(last, axis, up)  8.3 us
    conv_general_dilated x2, matrix products, convolve(): lax.conv_general_dilated(source, filters, (1, 1), ((0, 0), (1, 1)), dimen...  5.21 us
    unnamed x26, local copies, waits for them, and re-layouts  5.17 us
  transfers between devices with their start and end apart: 6, of which 3 were waited for; matrix products, arithmetic and copies ran while one was open for 28% of the time, Pallas kernels for 0%

commit v1 on v0

v1 whole, which is shorter than its diff:
```python
import functools
import math

import jax
import jax.numpy as jnp
from jax import lax
from jax.experimental import pallas as pl
from jax.experimental.pallas import tpu as pltpu
from jax.sharding import PartitionSpec as P

MESH = pl.DeviceIdType.MESH

OWN, UP, DOWN = 0, 1, 2


def shifted(x, by):
    width = x.shape[1]
    at = lax.broadcasted_iota(jnp.int32, x.shape, 1)
    edge = 0 if by > 0 else width - 1
    return jnp.where(at == edge, 0.0, pltpu.roll(x, by % width, 1))


def kernel(
    strips, scale, x_ref, g_ref, wf_ref, wb_ref, out_ref, ing_ref, kg_ref,
    x_buf, g_buf, taps_g, whole, pieces, landed, send_sem, recv_sem, kg_send, kg_recv, local_sem,
):
    own, height = x_ref.shape[1], x_ref.shape[0]
    channels = x_buf.shape[1]
    width = x_ref.shape[2]
    piece = kg_ref.shape[1]
    row = lax.axis_index("rows")
    chan = lax.axis_index("chan")
    sibling = chan + 1 - 2 * lax.rem(chan, 2)
    across = lax.rem(chan + 2, 4)
    diagonal = lax.rem(sibling + 2, 4)
    of = (chan, sibling, across, diagonal)
    bufs = (x_buf, g_buf)
    last = strips - 1
    span = {OWN: (1, height), UP: (0, 1), DOWN: (height + 1, 1)}

    def region(t, kind, channel):
        start, count = span[kind]
        return bufs[t].at[pl.ds(start, count), pl.ds(pl.multiple_of(channel * own, own), own), :]

    def relay(t, kind, held, to):
        where = region(t, kind, of[held])
        return pltpu.make_async_remote_copy(
            src_ref=where, dst_ref=where,
            send_sem=send_sem.at[t, kind, held ^ to], recv_sem=recv_sem.at[t, kind, held ^ to],
            device_id=(row, of[to]), device_id_type=MESH,
        )

    def edge(t, kind):
        at, to = (height, row + 1) if kind == UP else (1, row - 1)
        return pltpu.make_async_remote_copy(
            src_ref=bufs[t].at[pl.ds(at, 1), pl.ds(pl.multiple_of(chan * own, own), own), :],
            dst_ref=region(t, kind, chan),
            send_sem=send_sem.at[t, kind, 0], recv_sem=recv_sem.at[t, kind, 0],
            device_id=(to, chan), device_id_type=MESH,
        )

    def arrived(t, kind, held):
        where = region(t, kind, of[held])
        pltpu.make_async_remote_copy(
            src_ref=where, dst_ref=where,
            send_sem=send_sem.at[t, kind, held], recv_sem=recv_sem.at[t, kind, held],
            device_id=(row, sibling), device_id_type=MESH,
        ).wait_recv()

    has = {UP: row > 0, DOWN: row < last}
    feeds = {UP: row < last, DOWN: row > 0}

    mine = [
        pltpu.make_async_copy((x_ref, g_ref)[t], region(t, OWN, chan), local_sem.at[t])
        for t in range(2)
    ]
    for copy in mine:
        copy.start()

    barrier = pltpu.get_barrier_semaphore()
    for peer in (sibling, across):
        pl.semaphore_signal(barrier, inc=1, device_id=(row, peer), device_id_type=MESH)

    @pl.loop(1, strips)
    def _(d):
        pl.semaphore_signal(
            barrier, inc=1, device_id=(lax.rem(row + d, strips), chan), device_id_type=MESH
        )

    for kind, at in ((UP, 0), (DOWN, height + 1)):

        @pl.when(jnp.logical_not(has[kind]))
        def _():
            for t in range(2):
                bufs[t][at] = jnp.zeros((channels, width), jnp.bfloat16)

    for copy in mine:
        copy.wait()
    pl.semaphore_wait(barrier, strips + 1)

    for t in range(2):
        for kind in (UP, DOWN):

            @pl.when(feeds[kind])
            def _():
                edge(t, kind).start()

        relay(t, OWN, 0, 2).start()
        relay(t, OWN, 0, 1).start()

    for h in range(height):
        rows = g_ref[h].astype(jnp.float32)
        taps_g[h, 0:own] = shifted(rows, -1).astype(jnp.bfloat16)
        taps_g[h, own : 2 * own] = g_ref[h]
        taps_g[h, 2 * own : 3 * own] = shifted(rows, 1).astype(jnp.bfloat16)

    for t in range(2):
        for kind in (UP, DOWN):

            @pl.when(has[kind])
            def _():
                arrived(t, kind, 0)
                relay(t, kind, 0, 2).start()
                relay(t, kind, 0, 1).start()

        arrived(t, OWN, 2)
        relay(t, OWN, 2, 1).start()

    def pass_on(t):
        for kind in (UP, DOWN):

            @pl.when(has[kind])
            def _():
                arrived(t, kind, 2)
                relay(t, kind, 2, 1).start()

    def complete(t):
        arrived(t, OWN, 1)
        arrived(t, OWN, 3)
        for kind in (UP, DOWN):

            @pl.when(has[kind])
            def _():
                arrived(t, kind, 1)
                arrived(t, kind, 3)

    def stack(t, h):
        return bufs[t][h : h + 3].reshape(3 * channels, width)

    def convolve(t, w_ref, to_ref):
        for h in range(height):
            terms = jnp.dot(w_ref[...], stack(t, h), preferred_element_type=jnp.float32)
            total = (
                shifted(terms[0:own], 1) + terms[own : 2 * own] + shifted(terms[2 * own : 3 * own], -1)
            )
            to_ref[h] = total.astype(to_ref.dtype)

    pass_on(0)
    complete(0)
    terms = None
    for h in range(height):
        term = lax.dot_general(
            taps_g[h], stack(0, h), (((1,), (1,)), ((), ())), preferred_element_type=jnp.float32
        )
        terms = term if terms is None else terms + term
    for a in range(3):
        for b in range(3):
            whole[:, (3 * a + b) * channels : (3 * a + b + 1) * channels] = (
                terms[b * own : (b + 1) * own, a * channels : (a + 1) * channels] * scale
            )
    for s in range(strips):
        pieces[s] = whole[:, s * piece : (s + 1) * piece]

    def share(d):
        to = lax.rem(row + d, strips)
        return pltpu.make_async_remote_copy(
            src_ref=pieces.at[to], dst_ref=landed.at[d],
            send_sem=kg_send.at[d], recv_sem=kg_recv.at[d],
            device_id=(to, chan), device_id_type=MESH,
        )

    @pl.loop(1, strips)
    def _(d):
        share(d).start()

    pass_on(1)
    convolve(0, wf_ref, out_ref)
    complete(1)
    convolve(1, wb_ref, ing_ref)

    kg_ref[...] = pieces[row]

    @pl.loop(1, strips)
    def _(d):
        share(d).wait_recv()
        kg_ref[...] += landed[d]

    @pl.loop(1, strips)
    def _(d):
        share(d).wait_send()

    for t in range(2):
        relay(t, OWN, 0, 2).wait_send()
        relay(t, OWN, 0, 1).wait_send()
        relay(t, OWN, 2, 1).wait_send()
        for kind in (UP, DOWN):

            @pl.when(feeds[kind])
            def _():
                edge(t, kind).wait_send()

            @pl.when(has[kind])
            def _():
                relay(t, kind, 0, 2).wait_send()
                relay(t, kind, 0, 1).wait_send()
                relay(t, kind, 2, 1).wait_send()


def body(inputs, kernel_taps, out_grad):
    channels = kernel_taps.shape[0]
    own, height, width = inputs.shape
    strips = lax.axis_size("rows")
    piece = 9 * channels // strips
    first = lax.axis_index("chan") * own
    taps = kernel_taps.reshape(channels, 3, 3, channels)
    forward = lax.dynamic_slice_in_dim(taps, first, own, 0)
    forward = jnp.transpose(forward, (2, 0, 1, 3)).reshape(3 * own, 3 * channels)
    backward = lax.dynamic_slice_in_dim(taps, first, own, 3)[:, ::-1, ::-1, :]
    backward = jnp.transpose(backward, (2, 3, 1, 0)).reshape(3 * own, 3 * channels)
    scale = 1.0 / math.sqrt(height * strips * width)
    block = jax.ShapeDtypeStruct((height, own, width), jnp.bfloat16)
    vmem = pl.BlockSpec(memory_space=pltpu.VMEM)
    outputs, in_grad, kernel_grad = pl.pallas_call(
        functools.partial(kernel, strips, scale),
        out_shape=(block, block, jax.ShapeDtypeStruct((own, piece), jnp.float32)),
        in_specs=[vmem] * 4,
        out_specs=(vmem,) * 3,
        scratch_shapes=[
            pltpu.VMEM((height + 2, channels, width), jnp.bfloat16),
            pltpu.VMEM((height + 2, channels, width), jnp.bfloat16),
            pltpu.VMEM((height, 3 * own, width), jnp.bfloat16),
            pltpu.VMEM((own, 9 * channels), jnp.float32),
            pltpu.VMEM((strips, own, piece), jnp.float32),
            pltpu.VMEM((strips, own, piece), jnp.float32),
            pltpu.SemaphoreType.DMA((2, 3, 4)),
            pltpu.SemaphoreType.DMA((2, 3, 4)),
            pltpu.SemaphoreType.DMA((strips,)),
            pltpu.SemaphoreType.DMA((strips,)),
            pltpu.SemaphoreType.DMA((2,)),
        ],
        compiler_params=pltpu.CompilerParams(
            collective_id=0, has_side_effects=True, vmem_limit_bytes=40 * 1024 * 1024
        ),
    )(jnp.transpose(inputs, (1, 0, 2)), jnp.transpose(out_grad, (1, 0, 2)), forward, backward)
    return (jnp.transpose(outputs, (1, 0, 2)), jnp.transpose(in_grad, (1, 0, 2)), kernel_grad)


def solution(mesh):
    placed = (P("chan", "rows", None), P(), P("chan", "rows", None))
    return jax.shard_map(
        body,
        mesh=mesh,
        in_specs=placed,
        out_specs=(P("chan", "rows", None), P("chan", "rows", None), P("chan", "rows")),
        check_vma=False,
    )
```

time: 171 us -> 51.5 us (0.30); the launches traced: 168 us -> 51.3 us
  local copies, waits for them, and re-layouts: 57.3 us -> 5.62 us
  Pallas kernels: 0 us -> 45 us
  blocking collectives: 42.2 us -> 0 us
  matrix products: 21.1 us -> 0 us
  waiting for transfers between devices: 17.5 us -> 0 us
  between operations: 15 us -> 0.72 us
  starting transfers between devices: 12.4 us -> 0 us
  other arithmetic: 2.52 us -> 0 us
    pallas_call x0 -> x1, Pallas kernels: none -> 45 us  [body(): pl.pallas_call(functools.partial(kernel, strips, scale), out_shape=(block...]
    unnamed x1 -> x0, blocking collectives: 42.2 us -> none
    conv_general_dilated x9 -> x0, local copies, waits for them, and re-layouts: 23.8 us -> none  [convolve(): lax.conv_general_dilated(source, filters, (1, 1), ((0, 0), (1, 1)), dimen...]
    ppermute x4 -> x0, waiting for transfers between devices: 17.5 us -> none  [the longest x2 17.3 us: with_halo(): before = lax.ppermute(last, axis, up)]
    transpose x1 -> x0, matrix products: 15.9 us -> none  [body(): jnp.transpose(kernel_terms, (0, 2, 3, 1)).reshape(own_count, 9 * channels)]
    broadcast_in_dim x4 -> x0, local copies, waits for them, and re-layouts: 12.7 us -> none  [the longest x2 10.1 us: body(): padded_in[None]]
    ppermute x4 -> x0, starting transfers between devices: 12.3 us -> none  [the longest x2 8.3 us: with_halo(): before = lax.ppermute(last, axis, up)]
    conv_general_dilated x2 -> x0, matrix products: 5.21 us -> none  [convolve(): lax.conv_general_dilated(source, filters, (1, 1), ((0, 0), (1, 1)), dimen...]
  transfers between devices with their start and end apart: 6 -> 0, of which waited for: 3 -> 0; matrix products, arithmetic and copies ran while one was open for 28% -> 0% of each run, Pallas kernels for 0% -> 0%
where the time goes in v1:
time: 51.5 us; the launch traced here: 51.3 us
  Pallas kernels  45 us (87%)
  local copies, waits for them, and re-layouts  5.62 us (11%)
  between operations  0.72 us (1%)
    pallas_call x1, Pallas kernels, body(): pl.pallas_call(functools.partial(kernel, strips, scale), out_shape=(block...  45 us
    unnamed x10, local copies, waits for them, and re-layouts  4.64 us

profile of v1, /device:TPU:11, one launch (start us, length us, event | category | flops | bytes accessed | tf_op | source)
XLA Modules:
  0.0 51.3 jit_solution(14970030238962758211)
XLA Ops:
  0.6 1.6 %copy.14 = bf16[256,2304]{0,1:T(8,128)(2,1)S(1)} copy(bf16[256,2304]{1,0:T(8,128)(2,1)} %param.4) | data formatting | bytes 2359296 | tf_op args[1]
  2.3 0.3 copy.16
  2.6 0.0 copy-start
  2.6 0.0 copy-start.1
  2.6 0.2 dynamic-slice_bitcast_fusion
  2.9 0.3 copy.15
  3.2 0.3 copy-done
  3.5 0.1 copy-done.1
  3.6 0.1 copy_bitcast_fusion
  3.7 45.0 %shard_map.58 = (bf16[2,64,1024]{2,1,0:T(8,128)(2,1)S(1)}, bf16[2,64,1024]{2,1,0:T(8,128)(2,1)S(1)}, f32[64,288]{1,0:T(8,128)S(1)}) custom-call(bf16[2,64,1024]{2,1,0:T(8,128)(2,1)S(1)} %get-tuple-element.16.x_ref, bf16[2,64,1024]{2,1,0:T(8,128)(2,1)S(1)} %get-tuple-element.15.g_ref, bf16[192,768]{1,0:T(8,128)(2,1)S(1)} %bitcast.18, ...), custom_call_target="tpu_custom_call" | custom-call | tf_op jit(solution)/shard_map/pallas_call | solution.py:233
  48.7 1.0 %copy.17 = bf16[64,2,1024]{2,1,0:T(2,128)(2,1)} copy(bf16[64,2,1024]{2,0,1:T(8,128)(2,1)S(1)} %bitcast.20) | data formatting | bytes 524288
  49.7 1.0 %copy.18 = bf16[64,2,1024]{2,1,0:T(2,128)(2,1)} copy(bf16[64,2,1024]{2,0,1:T(8,128)(2,1)S(1)} %bitcast.19) | data formatting | bytes 524288
  50.7 0.6 %copy.24 = f32[64,288]{1,0:T(8,128)} copy(f32[64,288]{1,0:T(8,128)S(1)} %get-tuple-element.22) | data formatting | bytes 147456
  (4 shorter events, 0.1 us)
Async XLA Ops:
  2.6 1.0 %copy-start = (bf16[64,2,1024]{2,1,0:T(2,128)(2,1)S(1)}, bf16[64,2,1024]{2,1,0:T(2,128)(2,1)}, u32[]{:S(2)}) copy-start(bf16[64,2,1024]{2,1,0:T(2,128)(2,1)} %param.5) | copy-start | bytes 786436
  2.6 1.0 %copy-start.1 = (bf16[64,2,1024]{2,1,0:T(2,128)(2,1)S(1)}, bf16[64,2,1024]{2,1,0:T(2,128)(2,1)}, u32[]{:S(2)}) copy-start(bf16[64,2,1024]{2,1,0:T(2,128)(2,1)} %param.3) | copy-start | bytes 786436

commit v2 on v1

--- a/solution.py
+++ b/solution.py
@@ -21,8 +21,8 @@
 
 
 def kernel(
-    strips, scale, x_ref, g_ref, wf_ref, wb_ref, out_ref, ing_ref, kg_ref,
-    x_buf, g_buf, taps_g, whole, pieces, landed, send_sem, recv_sem, kg_send, kg_recv, local_sem,
+    strips, scale, x_ref, g_ref, taps_ref, out_ref, ing_ref, kg_ref,
+    x_buf, g_buf, forward, backward, turned, taps_g, whole, pieces, landed, total, send_sem, recv_sem, kg_send, kg_recv, local_sem,
 ):
     own, height = x_ref.shape[1], x_ref.shape[0]
     channels = x_buf.shape[1]
@@ -98,23 +98,18 @@
         copy.wait()
     pl.semaphore_wait(barrier, strips + 1)
 
-    for t in range(2):
+    def send_edges(t):
         for kind in (UP, DOWN):
 
             @pl.when(feeds[kind])
             def _():
                 edge(t, kind).start()
 
+    def send_own(t):
         relay(t, OWN, 0, 2).start()
         relay(t, OWN, 0, 1).start()
 
-    for h in range(height):
-        rows = g_ref[h].astype(jnp.float32)
-        taps_g[h, 0:own] = shifted(rows, -1).astype(jnp.bfloat16)
-        taps_g[h, own : 2 * own] = g_ref[h]
-        taps_g[h, 2 * own : 3 * own] = shifted(rows, 1).astype(jnp.bfloat16)
-
-    for t in range(2):
+    def relay_edges(t):
         for kind in (UP, DOWN):
 
             @pl.when(has[kind])
@@ -123,6 +118,7 @@
                 relay(t, kind, 0, 2).start()
                 relay(t, kind, 0, 1).start()
 
+    def relay_own(t):
         arrived(t, OWN, 2)
         relay(t, OWN, 2, 1).start()
 
@@ -134,9 +130,11 @@
                 arrived(t, kind, 2)
                 relay(t, kind, 2, 1).start()
 
-    def complete(t):
+    def complete_own(t):
         arrived(t, OWN, 1)
         arrived(t, OWN, 3)
+
+    def complete_edges(t):
         for kind in (UP, DOWN):
 
             @pl.when(has[kind])
@@ -155,21 +153,59 @@
             )
             to_ref[h] = total.astype(to_ref.dtype)
 
-    pass_on(0)
-    complete(0)
+    send_own(0)
+    send_edges(1)
+    send_edges(0)
+    send_own(1)
+
+    first = pl.multiple_of(chan * own, own)
+    pair = pl.multiple_of((chan // 2) * 2 * own, 2 * own)
+    for a in range(3):
+        for b in range(3):
+            at = (3 * a + b) * channels
+            forward[b * own : (b + 1) * own, a * channels : (a + 1) * channels] = taps_ref[
+                pl.ds(first, own), at : at + channels
+            ]
+            turned[...] = jnp.transpose(
+                taps_ref[:, pl.ds(at + pair, 2 * own)].astype(jnp.float32)
+            )
+            backward[
+                (2 - b) * own : (3 - b) * own, (2 - a) * channels : (3 - a) * channels
+            ] = turned[pl.ds(pl.multiple_of(lax.rem(chan, 2) * own, own), own), :].astype(jnp.bfloat16)
+
+    def offset_columns(p, rows):
+        wide = rows.astype(jnp.float32)
+        taps_g[p, 0:own] = shifted(wide, -1).astype(jnp.bfloat16)
+        taps_g[p, own : 2 * own] = rows
+        taps_g[p, 2 * own : 3 * own] = shifted(wide, 1).astype(jnp.bfloat16)
+
+    for h in range(height):
+        offset_columns(h + 1, g_ref[h])
+
+    relay_own(0)
+    relay_edges(1)
+    for p in (0, height + 1):
+        offset_columns(p, g_buf[p, pl.ds(first, own), :])
+    complete_own(0)
     terms = None
     for h in range(height):
         term = lax.dot_general(
-            taps_g[h], stack(0, h), (((1,), (1,)), ((), ())), preferred_element_type=jnp.float32
+            taps_g[h : h + 3].reshape(9 * own, width), x_buf[h + 1],
+            (((1,), (1,)), ((), ())), preferred_element_type=jnp.float32,
         )
         terms = term if terms is None else terms + term
     for a in range(3):
         for b in range(3):
+            at = (3 * (2 - a) + b) * own
             whole[:, (3 * a + b) * channels : (3 * a + b + 1) * channels] = (
-                terms[b * own : (b + 1) * own, a * channels : (a + 1) * channels] * scale
+                terms[at : at + own] * scale
             )
+    group = pieces.shape[1]
     for s in range(strips):
-        pieces[s] = whole[:, s * piece : (s + 1) * piece]
+        for q in range(own // group):
+            pieces[s, :, q * piece : (q + 1) * piece] = whole[
+                q * group : (q + 1) * group, s * piece : (s + 1) * piece
+            ]
 
     def share(d):
         to = lax.rem(row + d, strips)
@@ -183,17 +219,25 @@
     def _(d):
         share(d).start()
 
+    relay_edges(0)
+    relay_own(1)
     pass_on(1)
-    convolve(0, wf_ref, out_ref)
-    complete(1)
-    convolve(1, wb_ref, ing_ref)
-
-    kg_ref[...] = pieces[row]
+    pass_on(0)
+    complete_own(1)
+    complete_edges(1)
+    convolve(1, backward, ing_ref)
+    complete_edges(0)
+    convolve(0, forward, out_ref)
+
+    total[...] = pieces[row]
 
     @pl.loop(1, strips)
     def _(d):
         share(d).wait_recv()
-        kg_ref[...] += landed[d]
+        total[...] += landed[d]
+
+    for q in range(own // group):
+        kg_ref[q * group : (q + 1) * group, :] = total[:, q * piece : (q + 1) * piece]
 
     @pl.loop(1, strips)
     def _(d):
@@ -221,27 +265,28 @@
     own, height, width = inputs.shape
     strips = lax.axis_size("rows")
     piece = 9 * channels // strips
-    first = lax.axis_index("chan") * own
-    taps = kernel_taps.reshape(channels, 3, 3, channels)
-    forward = lax.dynamic_slice_in_dim(taps, first, own, 0)
-    forward = jnp.transpose(forward, (2, 0, 1, 3)).reshape(3 * own, 3 * channels)
-    backward = lax.dynamic_slice_in_dim(taps, first, own, 3)[:, ::-1, ::-1, :]
-    backward = jnp.transpose(backward, (2, 3, 1, 0)).reshape(3 * own, 3 * channels)
+    splits = [q for q in (1, 2, 4, 8) if own % (8 * q) == 0]
+    split = min(splits, key=lambda q: (own // q) * -(-q * piece // 128))
+    group, lanes = own // split, split * piece
     scale = 1.0 / math.sqrt(height * strips * width)
     block = jax.ShapeDtypeStruct((height, own, width), jnp.bfloat16)
     vmem = pl.BlockSpec(memory_space=pltpu.VMEM)
     outputs, in_grad, kernel_grad = pl.pallas_call(
         functools.partial(kernel, strips, scale),
         out_shape=(block, block, jax.ShapeDtypeStruct((own, piece), jnp.float32)),
-        in_specs=[vmem] * 4,
+        in_specs=[vmem] * 3,
         out_specs=(vmem,) * 3,
         scratch_shapes=[
             pltpu.VMEM((height + 2, channels, width), jnp.bfloat16),
             pltpu.VMEM((height + 2, channels, width), jnp.bfloat16),
-            pltpu.VMEM((height, 3 * own, width), jnp.bfloat16),
+            pltpu.VMEM((3 * own, 3 * channels), jnp.bfloat16),
+            pltpu.VMEM((3 * own, 3 * channels), jnp.bfloat16),
+            pltpu.VMEM((2 * own, channels), jnp.float32),
+            pltpu.VMEM((height + 2, 3 * own, width), jnp.bfloat16),
             pltpu.VMEM((own, 9 * channels), jnp.float32),
-            pltpu.VMEM((strips, own, piece), jnp.float32),
-            pltpu.VMEM((strips, own, piece), jnp.float32),
+            pltpu.VMEM((strips, group, lanes), jnp.float32),
+            pltpu.VMEM((strips, group, lanes), jnp.float32),
+            pltpu.VMEM((group, lanes), jnp.float32),
             pltpu.SemaphoreType.DMA((2, 3, 4)),
             pltpu.SemaphoreType.DMA((2, 3, 4)),
             pltpu.SemaphoreType.DMA((strips,)),
@@ -251,7 +296,7 @@
         compiler_params=pltpu.CompilerParams(
             collective_id=0, has_side_effects=True, vmem_limit_bytes=40 * 1024 * 1024
         ),
-    )(jnp.transpose(inputs, (1, 0, 2)), jnp.transpose(out_grad, (1, 0, 2)), forward, backward)
+    )(jnp.transpose(inputs, (1, 0, 2)), jnp.transpose(out_grad, (1, 0, 2)), kernel_taps)
     return (jnp.transpose(outputs, (1, 0, 2)), jnp.transpose(in_grad, (1, 0, 2)), kernel_grad)
 
 

time: 51.5 us -> 37.1 us (0.72)
  the two profiles are of different devices: /device:TPU:11 before, /device:TPU:3 now
where the time goes in v2:
time: 37.1 us; the launch traced here: 37 us
  Pallas kernels  31.3 us (84%)
  local copies, waits for them, and re-layouts  4.99 us (13%)
  between operations  0.66 us (2%)
    pallas_call x1, Pallas kernels, body(): pl.pallas_call(functools.partial(kernel, strips, scale), out_shape=(block...  31.3 us
    unnamed x5, local copies, waits for them, and re-layouts  3.85 us
    transpose x1, local copies, waits for them, and re-layouts, body(): jnp.transpose(out_grad, (1, 0, 2))  1.14 us

profile of v2, /device:TPU:3, one launch (start us, length us, event | category | flops | bytes accessed | tf_op | source)
XLA Modules:
  0.0 37.0 jit_solution(11987103902490343304)
XLA Ops:
  0.6 1.1 %copy_bitcast_fusion = (bf16[2,64,1024]{2,1,0:T(8,128)(2,1)S(1)}, bf16[2,64,1024]{2,1,0:T(8,128)(2,1)S(1)}) fusion(bf16[64,2,1024]{2,1,0:T(2,128)(2,1)} %param.5, bf16[64,2,1024]{2,1,0:T(2,128)(2,1)} %param.3), kind=kLoop, calls=%fused_computation | loop fusion | bytes 1048576 | tf_op jit(solution)/shard_map/transpose | solution.py:299
  1.8 0.0 copy-start
  1.8 1.3 %copy-done = bf16[256,2304]{1,0:T(8,128)(2,1)S(1)} copy-done((bf16[256,2304]{1,0:T(8,128)(2,1)S(1)}, bf16[256,2304]{1,0:T(8,128)(2,1)}, u32[]{:S(2)}) %copy-start) | copy-done | bytes 1179672
  3.1 31.3 %shard_map.58 = (bf16[2,64,1024]{2,1,0:T(8,128)(2,1)S(1)}, bf16[2,64,1024]{2,1,0:T(8,128)(2,1)S(1)}, f32[64,288]{1,0:T(8,128)S(1)}) custom-call(bf16[2,64,1024]{2,1,0:T(8,128)(2,1)S(1)} %get-tuple-element.13.x_ref, bf16[2,64,1024]{2,1,0:T(8,128)(2,1)S(1)} %get-tuple-element.12.g_ref, bf16[256,2304]{1,0:T(8,128)(2,1)S(1)} %copy-done), custom_call_target="tpu_custom_call" | custom-call | tf_op jit(solution)/shard_map/pallas_call | solution.py:274
  34.4 1.0 %copy.8 = bf16[64,2,1024]{2,1,0:T(2,128)(2,1)} copy(bf16[64,2,1024]{2,0,1:T(8,128)(2,1)S(1)} %bitcast.7) | data formatting | bytes 524288
  35.3 1.0 %copy.9 = bf16[64,2,1024]{2,1,0:T(2,128)(2,1)} copy(bf16[64,2,1024]{2,0,1:T(8,128)(2,1)S(1)} %bitcast.6) | data formatting | bytes 524288
  36.3 0.6 %copy.13 = f32[64,288]{1,0:T(8,128)} copy(f32[64,288]{1,0:T(8,128)S(1)} %get-tuple-element.19) | data formatting | bytes 147456
Async XLA Ops:
  1.8 1.3 %copy-start = (bf16[256,2304]{1,0:T(8,128)(2,1)S(1)}, bf16[256,2304]{1,0:T(8,128)(2,1)}, u32[]{:S(2)}) copy-start(bf16[256,2304]{1,0:T(8,128)(2,1)} %taps_ref.1) | copy-start | bytes 3538948

commit v3 on v2

--- a/solution.py
+++ b/solution.py
@@ -21,8 +21,8 @@
 
 
 def kernel(
-    strips, scale, x_ref, g_ref, taps_ref, out_ref, ing_ref, kg_ref,
-    x_buf, g_buf, forward, backward, turned, taps_g, whole, pieces, landed, total, send_sem, recv_sem, kg_send, kg_recv, local_sem,
+    strips, scale, x_ref, g_ref, taps_hbm, out_ref, ing_ref, kg_ref,
+    taps_ref, x_buf, g_buf, forward, backward, turned, taps_g, whole, pieces, landed, total, part, send_sem, recv_sem, kg_send, kg_recv, local_sem, near_sem,
 ):
     own, height = x_ref.shape[1], x_ref.shape[0]
     channels = x_buf.shape[1]
@@ -59,6 +59,15 @@
             device_id=(to, chan), device_id_type=MESH,
         )
 
+    def near_edge(t, kind):
+        at, to = (height, row + 1) if kind == UP else (1, row - 1)
+        return pltpu.make_async_remote_copy(
+            src_ref=bufs[t].at[pl.ds(at, 1), pl.ds(pl.multiple_of(across * own, own), own), :],
+            dst_ref=region(t, kind, across),
+            send_sem=near_sem.at[t], recv_sem=recv_sem.at[t, kind, 2],
+            device_id=(to, chan), device_id_type=MESH,
+        )
+
     def arrived(t, kind, held):
         where = region(t, kind, of[held])
         pltpu.make_async_remote_copy(
@@ -69,12 +78,20 @@
 
     has = {UP: row > 0, DOWN: row < last}
     feeds = {UP: row < last, DOWN: row > 0}
+    even = lax.rem(row, 2) == 0
+    near = {UP: jnp.logical_not(even), DOWN: even}
+    nears = {UP: even, DOWN: jnp.logical_not(even)}
+    direct = (0,)
+
+    def crosses(t, kind):
+        return jnp.logical_and(has[kind], jnp.logical_not(near[kind])) if t in direct else has[kind]
 
     mine = [
         pltpu.make_async_copy((x_ref, g_ref)[t], region(t, OWN, chan), local_sem.at[t])
         for t in range(2)
     ]
-    for copy in mine:
+    fetch = pltpu.make_async_copy(taps_hbm, taps_ref, local_sem.at[2])
+    for copy in (*mine, fetch):
         copy.start()
 
     barrier = pltpu.get_barrier_semaphore()
@@ -115,12 +132,21 @@
             @pl.when(has[kind])
             def _():
                 arrived(t, kind, 0)
+                relay(t, kind, 0, 1).start()
+
+            @pl.when(crosses(t, kind))
+            def _():
                 relay(t, kind, 0, 2).start()
-                relay(t, kind, 0, 1).start()
 
     def relay_own(t):
         arrived(t, OWN, 2)
         relay(t, OWN, 2, 1).start()
+        if t in direct:
+            for kind in (UP, DOWN):
+
+                @pl.when(nears[kind])
+                def _():
+                    near_edge(t, kind).start()
 
     def pass_on(t):
         for kind in (UP, DOWN):
@@ -142,12 +168,21 @@
                 arrived(t, kind, 1)
                 arrived(t, kind, 3)
 
-    def stack(t, h):
-        return bufs[t][h : h + 3].reshape(3 * channels, width)
-
-    def convolve(t, w_ref, to_ref):
+    def from_own(t, w_ref):
+        mid = bufs[t][1 : height + 1].reshape(height * channels, width)
         for h in range(height):
-            terms = jnp.dot(w_ref[...], stack(t, h), preferred_element_type=jnp.float32)
+            at = (1 - h) * channels
+            part[t, h] = jnp.dot(
+                w_ref[:, at : at + height * channels], mid, preferred_element_type=jnp.float32
+            )
+
+    def from_edges(t, w_ref, to_ref):
+        for h in range(height):
+            at = 2 * h * channels
+            terms = part[t, h] + jnp.dot(
+                w_ref[:, at : at + channels], bufs[t][h * (height + 1)],
+                preferred_element_type=jnp.float32,
+            )
             total = (
                 shifted(terms[0:own], 1) + terms[own : 2 * own] + shifted(terms[2 * own : 3 * own], -1)
             )
@@ -158,6 +193,7 @@
     send_edges(0)
     send_own(1)
 
+    fetch.wait()
     first = pl.multiple_of(chan * own, own)
     pair = pl.multiple_of((chan // 2) * 2 * own, 2 * own)
     for a in range(3):
@@ -221,13 +257,16 @@
 
     relay_edges(0)
     relay_own(1)
+    from_own(0, forward)
     pass_on(1)
+    complete_own(1)
     pass_on(0)
-    complete_own(1)
+    from_own(1, backward)
     complete_edges(1)
-    convolve(1, backward, ing_ref)
+    from_edges(1, backward, ing_ref)
+
     complete_edges(0)
-    convolve(0, forward, out_ref)
+    from_edges(0, forward, out_ref)
 
     total[...] = pieces[row]
 
@@ -253,9 +292,18 @@
             def _():
                 edge(t, kind).wait_send()
 
+            @pl.when(crosses(t, kind))
+            def _():
+                relay(t, kind, 0, 2).wait_send()
+
+            if t in direct:
+
+                @pl.when(nears[kind])
+                def _():
+                    near_edge(t, kind).wait_send()
+
             @pl.when(has[kind])
             def _():
-                relay(t, kind, 0, 2).wait_send()
                 relay(t, kind, 0, 1).wait_send()
                 relay(t, kind, 2, 1).wait_send()
 
@@ -274,9 +322,10 @@
     outputs, in_grad, kernel_grad = pl.pallas_call(
         functools.partial(kernel, strips, scale),
         out_shape=(block, block, jax.ShapeDtypeStruct((own, piece), jnp.float32)),
-        in_specs=[vmem] * 3,
+        in_specs=[vmem, vmem, pl.BlockSpec(memory_space=pltpu.HBM)],
         out_specs=(vmem,) * 3,
         scratch_shapes=[
+            pltpu.VMEM(kernel_taps.shape, jnp.bfloat16),
             pltpu.VMEM((height + 2, channels, width), jnp.bfloat16),
             pltpu.VMEM((height + 2, channels, width), jnp.bfloat16),
             pltpu.VMEM((3 * own, 3 * channels), jnp.bfloat16),
@@ -287,10 +336,12 @@
             pltpu.VMEM((strips, group, lanes), jnp.float32),
             pltpu.VMEM((strips, group, lanes), jnp.float32),
             pltpu.VMEM((group, lanes), jnp.float32),
+            pltpu.VMEM((2, height, 3 * own, width), jnp.float32),
             pltpu.SemaphoreType.DMA((2, 3, 4)),
             pltpu.SemaphoreType.DMA((2, 3, 4)),
             pltpu.SemaphoreType.DMA((strips,)),
             pltpu.SemaphoreType.DMA((strips,)),
+            pltpu.SemaphoreType.DMA((3,)),
             pltpu.SemaphoreType.DMA((2,)),
         ],
         compiler_params=pltpu.CompilerParams(

time: 37.1 us -> 36.3 us (0.978)
  the two profiles are of different devices: /device:TPU:3 before, /device:TPU:11 now
where the time goes in v3:
time: 36.3 us; the launch traced here: 36.1 us
  Pallas kernels  30.4 us (84%)
  local copies, waits for them, and re-layouts  4.99 us (14%)
  between operations  0.66 us (2%)
    pallas_call x1, Pallas kernels, body(): pl.pallas_call(functools.partial(kernel, strips, scale), out_shape=(block...  30.4 us
    unnamed x5, local copies, waits for them, and re-layouts  3.85 us
    transpose x1, local copies, waits for them, and re-layouts, body(): jnp.transpose(out_grad, (1, 0, 2))  1.14 us

profile of v3, /device:TPU:11, one launch (start us, length us, event | category | flops | bytes accessed | tf_op | source)
XLA Modules:
  0.0 36.1 jit_solution(5045278778426318904)
XLA Ops:
  0.6 1.1 %copy_bitcast_fusion = (bf16[2,64,1024]{2,1,0:T(8,128)(2,1)S(1)}, bf16[2,64,1024]{2,1,0:T(8,128)(2,1)S(1)}) fusion(bf16[64,2,1024]{2,1,0:T(2,128)(2,1)} %param.5, bf16[64,2,1024]{2,1,0:T(2,128)(2,1)} %param.3), kind=kLoop, calls=%fused_computation | loop fusion | bytes 1048576 | tf_op jit(solution)/shard_map/transpose | solution.py:350
  1.8 0.0 copy-start
  1.8 1.3 %copy-done = bf16[256,2304]{1,0:T(8,128)(2,1)S(1)} copy-done((bf16[256,2304]{1,0:T(8,128)(2,1)S(1)}, bf16[256,2304]{1,0:T(8,128)(2,1)}, u32[]{:S(2)}) %copy-start) | copy-done | bytes 1179672
  3.1 30.4 %shard_map.58 = (bf16[2,64,1024]{2,1,0:T(8,128)(2,1)S(1)}, bf16[2,64,1024]{2,1,0:T(8,128)(2,1)S(1)}, f32[64,288]{1,0:T(8,128)S(1)}) custom-call(bf16[2,64,1024]{2,1,0:T(8,128)(2,1)S(1)} %get-tuple-element.13.x_ref, bf16[2,64,1024]{2,1,0:T(8,128)(2,1)S(1)} %get-tuple-element.12.g_ref, bf16[256,2304]{1,0:T(8,128)(2,1)S(1)} %copy-done), custom_call_target="tpu_custom_call" | custom-call | tf_op jit(solution)/shard_map/pallas_call | solution.py:322
  33.5 1.0 %copy.8 = bf16[64,2,1024]{2,1,0:T(2,128)(2,1)} copy(bf16[64,2,1024]{2,0,1:T(8,128)(2,1)S(1)} %bitcast.7) | data formatting | bytes 524288
  34.5 1.0 %copy.9 = bf16[64,2,1024]{2,1,0:T(2,128)(2,1)} copy(bf16[64,2,1024]{2,0,1:T(8,128)(2,1)S(1)} %bitcast.6) | data formatting | bytes 524288
  35.4 0.6 %copy.13 = f32[64,288]{1,0:T(8,128)} copy(f32[64,288]{1,0:T(8,128)S(1)} %get-tuple-element.19) | data formatting | bytes 147456
Async XLA Ops:
  1.8 1.3 %copy-start = (bf16[256,2304]{1,0:T(8,128)(2,1)S(1)}, bf16[256,2304]{1,0:T(8,128)(2,1)}, u32[]{:S(2)}) copy-start(bf16[256,2304]{1,0:T(8,128)(2,1)} %taps_hbm.1) | copy-start | bytes 3538948

commit v4 on v3

--- a/solution.py
+++ b/solution.py
@@ -188,8 +188,8 @@
             )
             to_ref[h] = total.astype(to_ref.dtype)
 
+    send_edges(1)
     send_own(0)
-    send_edges(1)
     send_edges(0)
     send_own(1)
 
@@ -257,11 +257,11 @@
 
     relay_edges(0)
     relay_own(1)
+    pass_on(1)
     from_own(0, forward)
-    pass_on(1)
     complete_own(1)
+    from_own(1, backward)
     pass_on(0)
-    from_own(1, backward)
     complete_edges(1)
     from_edges(1, backward, ing_ref)
 

time: 36.3 us -> 36.3 us (level)
  no operation moved by 1% of the time
where the time goes in v4:
time: 36.3 us; the launch traced here: 36.1 us
  Pallas kernels  30.4 us (84%)
  local copies, waits for them, and re-layouts  4.99 us (14%)
  between operations  0.66 us (2%)
    pallas_call x1, Pallas kernels, body(): pl.pallas_call(functools.partial(kernel, strips, scale), out_shape=(block...  30.4 us
    unnamed x5, local copies, waits for them, and re-layouts  3.85 us
    transpose x1, local copies, waits for them, and re-layouts, body(): jnp.transpose(out_grad, (1, 0, 2))  1.14 us

profile of v4, /device:TPU:11, one launch (start us, length us, event | category | flops | bytes accessed | tf_op | source)
XLA Modules:
  0.0 36.1 jit_solution(2047751226708335721)
XLA Ops:
  0.6 1.1 %copy_bitcast_fusion = (bf16[2,64,1024]{2,1,0:T(8,128)(2,1)S(1)}, bf16[2,64,1024]{2,1,0:T(8,128)(2,1)S(1)}) fusion(bf16[64,2,1024]{2,1,0:T(2,128)(2,1)} %param.5, bf16[64,2,1024]{2,1,0:T(2,128)(2,1)} %param.3), kind=kLoop, calls=%fused_computation | loop fusion | bytes 1048576 | tf_op jit(solution)/shard_map/transpose | solution.py:350
  1.8 0.0 copy-start
  1.8 1.3 %copy-done = bf16[256,2304]{1,0:T(8,128)(2,1)S(1)} copy-done((bf16[256,2304]{1,0:T(8,128)(2,1)S(1)}, bf16[256,2304]{1,0:T(8,128)(2,1)}, u32[]{:S(2)}) %copy-start) | copy-done | bytes 1179672
  3.1 30.4 %shard_map.58 = (bf16[2,64,1024]{2,1,0:T(8,128)(2,1)S(1)}, bf16[2,64,1024]{2,1,0:T(8,128)(2,1)S(1)}, f32[64,288]{1,0:T(8,128)S(1)}) custom-call(bf16[2,64,1024]{2,1,0:T(8,128)(2,1)S(1)} %get-tuple-element.13.x_ref, bf16[2,64,1024]{2,1,0:T(8,128)(2,1)S(1)} %get-tuple-element.12.g_ref, bf16[256,2304]{1,0:T(8,128)(2,1)S(1)} %copy-done), custom_call_target="tpu_custom_call" | custom-call | tf_op jit(solution)/shard_map/pallas_call | solution.py:322
  33.5 1.0 %copy.8 = bf16[64,2,1024]{2,1,0:T(2,128)(2,1)} copy(bf16[64,2,1024]{2,0,1:T(8,128)(2,1)S(1)} %bitcast.7) | data formatting | bytes 524288
  34.5 1.0 %copy.9 = bf16[64,2,1024]{2,1,0:T(2,128)(2,1)} copy(bf16[64,2,1024]{2,0,1:T(8,128)(2,1)S(1)} %bitcast.6) | data formatting | bytes 524288
  35.4 0.6 %copy.13 = f32[64,288]{1,0:T(8,128)} copy(f32[64,288]{1,0:T(8,128)S(1)} %get-tuple-element.19) | data formatting | bytes 147456
Async XLA Ops:
  1.8 1.3 %copy-start = (bf16[256,2304]{1,0:T(8,128)(2,1)S(1)}, bf16[256,2304]{1,0:T(8,128)(2,1)}, u32[]{:S(2)}) copy-start(bf16[256,2304]{1,0:T(8,128)(2,1)} %taps_hbm.1) | copy-start | bytes 3538948
